TPU v7x, 256 devices: a whole 4x4x8 slice. The times are simulated.
256 devices in a mesh: hst: 4 (over x), chip: 64 (over z, y, core).
Axes of the slice: x: 4, y: 4, z: 8, core: 2. Of those that a mesh axis runs over, the one named last changes fastest.
Arguments:
- inputs: bfloat16 [262144, 4096], P(('hst', 'chip')), may hold values from -6 to 6, as said below
- out_grads: bfloat16 [262144, 1024], P(('hst', 'chip')), may hold values from -4 to 4, as said below
Outputs:
- weight_grad: float32 [4096, 1024], P(('hst', 'chip'))
Inputs may be any that keep to these rules, and one draw needn't show every extreme that they name: `inputs`: whole numbers. `out_grads`: whole numbers.
All inputs are finite; a program needn't handle non-finite values. Where the computation divides by a largest or mean magnitude, that divisor is 1e-20 or more.
Results may differ from a plain program's by a relative error of at most 0.0003.
Values may be sent and summed in bfloat16 or wider, within the bound.
A program may use at most 128 MiB of HBM per device.

v0:
```python
import jax
import jax.numpy as jnp
from jax import lax
from jax.sharding import PartitionSpec as P

BLOCK = 128


powers_list = [2.0**k for k in range(31)]
doubled_list = [2.0 ** (k + 1) for k in range(31)]


def hadamard_table(length):
    index = jnp.arange(length, dtype=jnp.int32)
    common = jnp.bitwise_and(index[:, None], index[None, :])
    parity = jnp.zeros((length, length), jnp.int32)
    for bit_number in range(length.bit_length() - 1):
        parity = parity + jnp.bitwise_and(jnp.right_shift(common, bit_number), 1)
    return 1.0 - 2.0 * (parity % 2).astype(jnp.float32)


def block_scale(largest):
    powers = jnp.array(powers_list, dtype=jnp.float32)
    doubled = jnp.array(doubled_list, dtype=jnp.float32)
    picked = jnp.where(largest[..., None] >= powers, doubled, jnp.ones_like(doubled))
    return jnp.max(picked, axis=-1) / 128.0


def quantize_last(values):
    scales = block_scale(jnp.max(jnp.abs(values), axis=-1))
    codes = jnp.floor(values / scales[..., None] + 0.5).astype(jnp.bfloat16)
    return (codes, scales)


def dequantize_last(codes, scales):
    return codes.astype(jnp.float32) * scales[..., None]


def body(inputs, out_grads):
    table = hadamard_table(BLOCK)
    hosts = lax.axis_size("hst")
    chips = lax.axis_size("chip")
    din = inputs.shape[1]
    width = out_grads.shape[1]
    blocks = width // BLOCK
    rows = din // (hosts * chips)
    token_count = inputs.shape[0] * hosts * chips
    local = lax.dot_general(
        inputs, out_grads, (((0,), (0,)), ((), ())), preferred_element_type=jnp.float32
    )
    rotated = jnp.einsum(
        "dbj,jk->dbk", local.reshape(din, blocks, BLOCK), table, precision=lax.Precision.HIGHEST
    )
    codes, scales = quantize_last(rotated)
    codes = codes.reshape(hosts, chips, rows, width)
    scales = scales.reshape(hosts, chips, rows, blocks)
    got_codes, got_scales = (
        lax.all_to_all(codes, "chip", split_axis=1, concat_axis=1, tiled=True),
        lax.all_to_all(
            scales.astype(jnp.bfloat16), "chip", split_axis=1, concat_axis=1, tiled=True
        ).astype(scales.dtype),
    )
    count = got_codes.shape[0]
    shaped = got_codes.reshape(count, chips, rows, blocks, BLOCK)
    partial_value = jnp.sum(dequantize_last(shaped, got_scales), axis=1)
    count = partial_value.shape[0]
    new_codes, new_scales = quantize_last(partial_value)
    codes2 = new_codes.reshape(count, rows, width)
    own_codes, own_scales = (
        lax.all_to_all(codes2, "hst", split_axis=0, concat_axis=0, tiled=True),
        lax.all_to_all(
            new_scales.astype(jnp.bfloat16), "hst", split_axis=0, concat_axis=0, tiled=True
        ).astype(new_scales.dtype),
    )
    shaped = own_codes.reshape(hosts, rows, blocks, BLOCK)
    total = jnp.sum(dequantize_last(shaped, own_scales), axis=0)
    result = jnp.einsum("rbj,jk->rbk", total, table, precision=lax.Precision.HIGHEST)
    factor = 1.0 / (512.0 * jnp.sqrt(jnp.float32(token_count)))
    return result.reshape(rows, width) * factor


def solution(mesh):
    placed = (P(("hst", "chip"), None), P(("hst", "chip"), None))
    return jax.shard_map(
        body, mesh=mesh, in_specs=placed, out_specs=P(("hst", "chip"), None), check_vma=False
    )
```

profile of v0, /device:TPU:16, one launch (start us, length us, event | category | flops | bytes accessed | tf_op | source)
XLA Modules:
  0.0 332.9 jit_solution(14105308626665567084)
XLA Ops:
  0.0 1.6 copy-done
  1.6 14.5 %fusion.46 = f32[4096,1024]{0,1:T(8,128)} fusion(bf16[1024,4096]{1,0:T(8,128)(2,1)} %param.6, bf16[1024,1024]{1,0:T(8,128)(2,1)S(1)} %copy-done), kind=kOutput, calls=%fused_computation.60 | convolution fusion | flops 8589934592 | bytes 27262976 | tf_op jit(solution)/shard_map/dot_general | solution.py:48
  16.1 31.6 %abs_reduce_fusion = (f32[4096,8]{0,1:T(8,128)S(1)}, f32[4096,8,128]{0,2,1:T(8,128)}) fusion(f32[4096,8,128]{0,2,1:T(8,128)} %bitcast.38), kind=kOutput, calls=%fused_computation.2 | convolution fusion | flops 6451380224 | bytes 33685504 | tf_op jit(solution)/shard_map/dbj,jk->dbk/dot_general | solution.py:51
  47.7 0.5 select_reduce_fusion
  49.0 1.1 reshape.41
  50.1 12.0 %all-to-all-start.1 = ((bf16[64,2,256]{2,1,0:T(2,128)(2,1)}), bf16[64,2,256]{2,1,0:T(2,128)(2,1)S(1)}, u32[]{:S(2)}, u32[]{:S(2)}) async-start(bf16[64,2,256]{2,1,0:T(2,128)(2,1)} %reshape.41), calls=%async_computation.1 | async-start | bytes 131072 | tf_op jit(solution)/shard_map/all_to_all | solution.py:59
  62.1 9.7 %floor_convert_fusion = bf16[4096,8,128]{0,2,1:T(8,128)(2,1)} fusion(f32[4096,8,128]{0,2,1:T(8,128)} %get-tuple-element.10, f32[4096,8]{0,1:T(8,128)S(1)} %get-tuple-element.5), kind=kLoop, calls=%fused_computation.1 | loop fusion | flops 16777216 | bytes 25296896 | tf_op jit(solution)/shard_map/convert_element_type | solution.py:31
  71.9 12.1 %copy.32 = bf16[4096,8,128]{2,1,0:T(8,128)(2,1)} copy(bf16[4096,8,128]{0,2,1:T(8,128)(2,1)} %floor_convert_fusion) | data formatting | bytes 16777216 | tf_op jit(solution)/shard_map/convert_element_type | solution.py:31
  83.9 13.3 %reshape.38 = bf16[4,64,16,1024]{3,2,1,0:T(8,128)(2,1)} reshape(bf16[4096,8,128]{2,1,0:T(8,128)(2,1)} %copy.32) | data formatting | bytes 16777216 | tf_op jit(solution)/shard_map/reshape | solution.py:55
  97.2 8.5 %copy.33 = bf16[4,64,16,1024]{3,2,0,1:T(8,128)(2,1)} copy(bf16[4,64,16,1024]{3,2,1,0:T(8,128)(2,1)} %reshape.38) | data formatting | bytes 16777216 | tf_op jit(solution)/shard_map/reshape | solution.py:55
  105.7 10.5 %all-to-all-start = ((bf16[4,64,16,1024]{3,2,0,1:T(8,128)(2,1)}), bf16[4,64,16,1024]{3,2,0,1:T(8,128)(2,1)}, u32[]{:S(2)}, u32[]{:S(2)}) async-start(bf16[4,64,16,1024]{3,2,0,1:T(8,128)(2,1)} %copy.33), calls=%async_computation | async-start | bytes 16777216 | tf_op jit(solution)/shard_map/all_to_all | solution.py:58
  116.6 0.6 copy.35
  117.2 1.7 copy.36
  118.9 8.5 %mul.41 = f32[4,64,16,8,128]{4,3,2,0,1:T(8,128)} broadcast(f32[4,64,16,8]{3,2,0,1:T(8,128)S(1)} %copy.36), dimensions={0,1,2,3} | broadcast | bytes 16908288 | tf_op jit(solution)/shard_map/mul | solution.py:36
  127.4 18.0 %mul.42 = f32[4,64,16,1024]{3,2,0,1:T(8,128)} reshape(f32[4,64,16,8,128]{4,3,2,0,1:T(8,128)} %mul.41) | data formatting | bytes 33554432 | tf_op jit(solution)/shard_map/mul | solution.py:36
  145.4 157.3 %all-to-all-done = bf16[4,64,16,1024]{3,2,0,1:T(8,128)(2,1)} async-done(((bf16[4,64,16,1024]{3,2,0,1:T(8,128)(2,1)}), bf16[4,64,16,1024]{3,2,0,1:T(8,128)(2,1)}, u32[]{:S(2)}, u32[]{:S(2)}) %all-to-all-start) | async-done | bytes 8388640 | tf_op jit(solution)/shard_map/all_to_all | solution.py:58
  302.6 9.3 %multiply_reduce_fusion = f32[4,16,1024]{2,1,0:T(8,128)S(1)} fusion(f32[4,64,16,1024]{3,2,0,1:T(8,128)} %mul.42, bf16[4,64,16,1024]{3,2,0,1:T(8,128)(2,1)} %all-to-all-done), kind=kLoop, calls=%fused_computation | loop fusion | flops 12517376 | bytes 25427968 | tf_op jit(solution)/shard_map/reduce_sum | solution.py:65
  312.4 0.7 copy.37
  313.1 4.3 %all-to-all-start.3 = ((bf16[4,16,8]{1,2,0:T(8,128)(2,1)}), bf16[4,16,8]{1,2,0:T(8,128)(2,1)S(1)}, u32[]{:S(2)}, u32[]{:S(2)}) async-start(bf16[4,16,8]{1,2,0:T(8,128)(2,1)} %copy.37), calls=%async_computation.3 | async-start | bytes 16384 | tf_op jit(solution)/shard_map/all_to_all | solution.py:71
  317.6 0.7 floor_convert_fusion.1
  318.2 4.4 %all-to-all-done.3 = bf16[4,16,8]{1,2,0:T(8,128)(2,1)S(1)} async-done(((bf16[4,16,8]{1,2,0:T(8,128)(2,1)}), bf16[4,16,8]{1,2,0:T(8,128)(2,1)S(1)}, u32[]{:S(2)}, u32[]{:S(2)}) %all-to-all-start.3) | async-done | bytes 1056 | tf_op jit(solution)/shard_map/all_to_all | solution.py:71
  322.7 3.3 all-to-all-start.2
  326.3 5.7 %all-to-all-done.2 = bf16[4,16,1024]{2,1,0:T(8,128)(2,1)S(1)} async-done(((bf16[4,16,1024]{2,1,0:T(8,128)(2,1)}), bf16[4,16,1024]{2,1,0:T(8,128)(2,1)S(1)}, u32[]{:S(2)}, u32[]{:S(2)}) %all-to-all-start.2) | async-done | bytes 131104 | tf_op jit(solution)/shard_map/all_to_all | solution.py:70
  332.3 0.6 copy.47
  (25 shorter events, 2.4 us)
Async XLA Ops:
  0.0 1.6 copy-start
  16.1 31.6 %copy-start.2 = (f32[31]{0:T(128)S(1)}, f32[31]{0:T(128)}, u32[]{:S(2)}) copy-start(f32[31]{0:T(128)} %constant.50.clone) | copy-start | bytes 376
  16.1 31.6 %copy-start.3 = (f32[31]{0:T(128)S(1)}, f32[31]{0:T(128)}, u32[]{:S(2)}) copy-start(f32[31]{0:T(128)} %constant.49.clone) | copy-start | bytes 376
  50.1 55.6 %all-to-all-start.1 = ((bf16[64,2,256]{2,1,0:T(2,128)(2,1)}), bf16[64,2,256]{2,1,0:T(2,128)(2,1)S(1)}, u32[]{:S(2)}, u32[]{:S(2)}) async-start(bf16[64,2,256]{2,1,0:T(2,128)(2,1)} %reshape.41), calls=%async_computation.1 | async-start | bytes 131072 | tf_op jit(solution)/shard_map/all_to_all | solution.py:59
  105.7 196.9 %all-to-all-start = ((bf16[4,64,16,1024]{3,2,0,1:T(8,128)(2,1)}), bf16[4,64,16,1024]{3,2,0,1:T(8,128)(2,1)}, u32[]{:S(2)}, u32[]{:S(2)}) async-start(bf16[4,64,16,1024]{3,2,0,1:T(8,128)(2,1)} %copy.33), calls=%async_computation | async-start | bytes 16777216 | tf_op jit(solution)/shard_map/all_to_all | solution.py:58
  302.6 30.3 %copy-start.1 = (bf16[1024,1024]{1,0:T(8,128)(2,1)S(1)}, bf16[1024,1024]{1,0:T(8,128)(2,1)}, u32[]{:S(2)}) copy-start(bf16[1024,1024]{1,0:T(8,128)(2,1)} %param.7) | copy-start | bytes 6291460
  313.1 9.6 %all-to-all-start.3 = ((bf16[4,16,8]{1,2,0:T(8,128)(2,1)}), bf16[4,16,8]{1,2,0:T(8,128)(2,1)S(1)}, u32[]{:S(2)}, u32[]{:S(2)}) async-start(bf16[4,16,8]{1,2,0:T(8,128)(2,1)} %copy.37), calls=%async_computation.3 | async-start | bytes 16384 | tf_op jit(solution)/shard_map/all_to_all | solution.py:71
  322.7 9.3 %all-to-all-start.2 = ((bf16[4,16,1024]{2,1,0:T(8,128)(2,1)}), bf16[4,16,1024]{2,1,0:T(8,128)(2,1)S(1)}, u32[]{:S(2)}, u32[]{:S(2)}) async-start(bf16[4,16,1024]{2,1,0:T(8,128)(2,1)} %floor_convert_fusion.1), calls=%async_computation.2 | async-start | bytes 262144 | tf_op jit(solution)/shard_map/all_to_all | solution.py:70
where the time goes:
time: 334 us; the launch traced here: 333 us
  waiting for transfers between devices  167 us (50%)
  local copies, waits for them, and re-layouts  68.3 us (20%)
  matrix products  46.4 us (14%)
  starting transfers between devices  30.1 us (9%)
  other arithmetic  20.7 us (6%)
    all_to_all x1, waiting for transfers between devices, body(): lax.all_to_all(codes, 'chip', split_axis=1, concat_axis=1, tiled=True)  157 us
    dot_general x1, matrix products, body(): jnp.einsum('dbj,jk->dbk', local.reshape(din, blocks, BLOCK), table, preci...  31.6 us
    mul x4, local copies, waits for them, and re-layouts, dequantize_last(): return codes.astype(jnp.float32) * scales[..., None]  26.6 us
    reshape x2, local copies, waits for them, and re-layouts, body(): codes = codes.reshape(hosts, chips, rows, width)  21.8 us
    dot_general x1, matrix products, body(): lax.dot_general(inputs, out_grads, (((0,), (0,)), ((), ())), preferred_el...  14.5 us
    convert_element_type x1, local copies, waits for them, and re-layouts, quantize_last(): codes = jnp.floor(values / scales[..., None] + 0.5).astype(jnp.bfloat16)  12.1 us
    all_to_all x1, starting transfers between devices, body(): lax.all_to_all(scales.astype(jnp.bfloat16), 'chip', split_axis=1, concat_...  12 us
    all_to_all x1, starting transfers between devices, body(): lax.all_to_all(codes, 'chip', split_axis=1, concat_axis=1, tiled=True)  10.5 us
  transfers between devices with their start and end apart: 4, of which 3 were waited for; matrix products, arithmetic and copies ran while one was open for 22% of the time, Pallas kernels for 0%

commit v1 on v0

v1 whole, which is shorter than its diff:
```python
import functools
import math

import jax
import jax.numpy as jnp
from jax import lax
from jax.experimental import pallas as pl
from jax.experimental.pallas import tpu as pltpu
from jax.sharding import PartitionSpec as P

MESH = pl.DeviceIdType.MESH
F32 = jnp.float32
BF16 = jnp.bfloat16
BLOCK = 128
HALF = BLOCK // 2
NX, NZ, NY, NK = 4, 8, 4, 2
TILES = NX
WIDE = TILES * BLOCK
SPLIT = 48
TALL = BLOCK - SPLIT
CHAIN = ((0, 1, 3, 5, 7), (0, 2, 4, 6, 7))
QCHAIN = ((0, 1, 3), (0, 2, 3))


def signs(upper):
    i = lax.broadcasted_iota(jnp.int32, (BLOCK, BLOCK), 0)
    j = lax.broadcasted_iota(jnp.int32, (BLOCK, BLOCK), 1)
    t = i & j
    if not upper:
        t = t & (HALF - 1)
    t = t ^ (t >> 4)
    t = t ^ (t >> 2)
    t = t ^ (t >> 1)
    value = (1 - 2 * (t & 1)).astype(F32)
    if not upper:
        value = jnp.where((i & HALF) == (j & HALF), value, 0.0)
    return value


def scale_pair(largest, count):
    scale = jnp.full_like(largest, 1.0 / 128.0)
    inverse = jnp.full_like(largest, 128.0)
    for k in range(count):
        above = largest >= 2.0**k
        scale = jnp.where(above, 2.0 ** (k + 1) / 128.0, scale)
        inverse = jnp.where(above, 128.0 / 2.0 ** (k + 1), inverse)
    return scale, inverse


def rounded_halves(w_ref, put):
    tops = []
    for j in range(NY):
        u = w_ref[j * BLOCK : j * BLOCK + HALF]
        v = w_ref[j * BLOCK + HALF : (j + 1) * BLOCK]
        tops.append(jnp.max(jnp.abs(u) + jnp.abs(v), axis=0, keepdims=True))
    scale, inverse = scale_pair(jnp.concatenate(tops, axis=0), 22)
    for j in range(NY):
        s, inv = scale[j : j + 1], inverse[j : j + 1]
        u = w_ref[j * BLOCK : j * BLOCK + HALF] * inv
        v = w_ref[j * BLOCK + HALF : (j + 1) * BLOCK] * inv
        put(j, 0, jnp.floor(u + v + 0.5) * s)
        put(j, HALF, jnp.floor(u - v + 0.5) * s)


def kernel(
    factor, a_ref, g_ref, out_ref,
    abuf, gbuf, gt, w0, w1, S, CS, CR, RY0, RY1, RZ0, RZ1, RZ20, RZ21, RY20, RY21, XC, XR, OT, OB,
    a_sem, g_sem, sib_s, sib_r, y1_s, y1_r, z1_s, z1_r, z2_s, z2_r, y2_s, y2_r, x_s, x_r, f_s, f_r,
):
    x = lax.axis_index("hst")
    c = lax.axis_index("chip")
    z, y, k = c // 8, (c // 2) % 4, c % 2

    def dev(x_, z_, y_, k_):
        return (x_, (z_ * NY + y_) * NK + k_)

    sibling = dev(x, z, y, 1 - k)
    y_next = (dev(x, z, (y + 1) % 4, k), dev(x, z, (y + 3) % 4, k))
    z_next = (dev(x, (z + 1) % 8, y, k), dev(x, (z + 7) % 8, y, k))
    place = y * 2 + k

    def mate(d):
        return (x, z * 8 + (place + d) % 8)

    def host(r):
        return ((x + r) % 4, c)

    def g_copy():
        return pltpu.make_async_copy(g_ref, gbuf, g_sem)

    def a_copy(i, r):
        off = jnp.where(i % 2 == 0, 4 + i // 2, 3 - i // 2)
        start = (((x + r) % 4) * 8 + (z + off) % 8) * BLOCK
        return pltpu.make_async_copy(
            a_ref.at[:, pl.ds(pl.multiple_of(start, BLOCK), BLOCK)],
            abuf.at[i, :, pl.ds(r * BLOCK, BLOCK)],
            a_sem.at[i, r],
        )

    g_copy().start()

    def start_a(i, carry):
        for r in range(TILES):
            a_copy(i, r).start()
        return carry

    lax.fori_loop(0, 8, start_a, 0)

    barrier = pltpu.get_barrier_semaphore()
    friends = [z_next[0], z_next[1]] + [host(r) for r in range(1, 4)] + [mate(d) for d in range(1, 8)]
    for friend in friends:
        pl.semaphore_signal(barrier, inc=1, device_id=friend, device_id_type=MESH)

    def remote(src, dst, ss, rs, to):
        return pltpu.make_async_remote_copy(
            src_ref=src, dst_ref=dst, send_sem=ss, recv_sem=rs, device_id=to, device_id_type=MESH
        )

    def sib_copy(i):
        return remote(CS.at[i], CR.at[i], sib_s.at[i], sib_r.at[i], sibling)

    def half(d):
        return pl.ds(d * (WIDE // 2), WIDE // 2)

    low, high = pl.ds(0, SPLIT), pl.ds(SPLIT, TALL)

    def y1_copy(i, d, s):
        if s == 0:
            src, dst = S.at[i, 0, high, half(d)], RY0.at[d, i]
        else:
            src, dst = S.at[i, QCHAIN[d][1], high, :], RY1.at[d, i]
        return remote(src, dst, y1_s.at[d, s, i], y1_r.at[d, s, i], y_next[d])

    def z1_copy(d, s, u):
        qs = pl.ds(2 * u, 2)
        if s == 0:
            src, dst = S.at[0, qs, low, half(d)], RZ0.at[d, u]
        else:
            src, dst = S.at[CHAIN[d][s], qs, low, :], RZ1.at[d, s - 1, u]
        return remote(src, dst, z1_s.at[d, s, u], z1_r.at[d, s, u], z_next[d])

    def z2_copy(d, s):
        if s == 0:
            src, dst = S.at[0, 3, high, half(d)], RZ20.at[d]
        else:
            src, dst = S.at[CHAIN[d][s], 3, high, :], RZ21.at[d, s - 1]
        return remote(src, dst, z2_s.at[d, s], z2_r.at[d, s], z_next[d])

    def y2_copy(d, s):
        if s == 0:
            src, dst = S.at[7, 0, low, half(d)], RY20.at[d]
        else:
            src, dst = S.at[7, QCHAIN[d][1], low, :], RY21.at[d]
        return remote(src, dst, y2_s.at[d, s], y2_r.at[d, s], y_next[d])

    def x_copy(r):
        return remote(XC.at[r], XR.at[r], x_s.at[r], x_r.at[r], host(r))

    def f_copy(d):
        rows = pl.ds(pl.multiple_of(((place + d) % 8) * 16, 16), 16)
        columns = pl.ds(pl.multiple_of(place * BLOCK, BLOCK), BLOCK)
        return remote(OT.at[rows, :], OB.at[:, columns], f_s.at[d], f_r.at[d], mate(d))

    def y1_first(i):
        for d in range(2):
            y1_copy(i, d, 0).wait_recv()
            q = QCHAIN[d][1]
            S[i, q, high, half(d)] += RY0[d, i]
            y1_copy(i, d, 1).start()

    def y1_last(i):
        for d in range(2):
            y1_copy(i, d, 1).wait_recv()
        S[i, 3, high, :] += RY1[0, i] + RY1[1, i]

    def z1_take(d, s):
        for u in range(2):
            z1_copy(d, s, u).wait_recv()
            slot = CHAIN[d][s + 1]
            if s == 0:
                S[slot, pl.ds(2 * u, 2), low, half(d)] += RZ0[d, u]
            else:
                S[slot, pl.ds(2 * u, 2), low, :] += RZ1[d, s - 1, u]
            if s < 3:
                z1_copy(d, s + 1, u).start()

    def z2_take(d, s):
        z2_copy(d, s).wait_recv()
        slot = CHAIN[d][s + 1]
        if s == 0:
            S[slot, 3, high, half(d)] += RZ20[d]
        else:
            S[slot, 3, high, :] += RZ21[d, s - 1]
        if s < 3:
            z2_copy(d, s + 1).start()

    g_copy().wait()
    table = signs(False).astype(BF16)
    for h in range(2):
        for q, off in enumerate((2, 1, 3, 0)):
            block = ((y + off) % 4) * 2 + (1 - k if h == 0 else k)
            columns = pl.ds(pl.multiple_of(block * BLOCK, BLOCK), BLOCK)
            turned = lax.dot_general(
                table, gbuf[:, columns], (((1,), (1,)), ((), ())), preferred_element_type=F32
            )
            start = h * 512 + q * BLOCK
            gt[start : start + BLOCK, :] = turned.astype(BF16)

    pl.semaphore_wait(barrier, len(friends))

    def own(i):
        def put(j, r, value):
            S[i, j, r : r + HALF, :] = value

        rounded_halves(w1, put)

    def finish(i):
        sib_copy(i).wait_recv()
        for q in range(NY):
            S[i, q] += CR[i, q].astype(F32)
        for d in range(2):
            y1_copy(i, d, 0).start()

    def step(i, carry):
        for r in range(TILES):
            a_copy(i, r).wait()
        w0[...] = jnp.dot(gt[0:512, :], abuf[i], preferred_element_type=F32)
        own(jnp.maximum(i - 1, 0))

        @pl.when(i >= 1)
        def _():
            finish(i - 1)

        @pl.when(i == 1)
        def _():
            for u in range(2):
                for d in range(2):
                    z1_copy(d, 0, u).start()

        @pl.when(i == 5)
        def _():
            for d in range(2):
                z1_take(d, 0)

        w1[...] = jnp.dot(gt[512:1024, :], abuf[i], preferred_element_type=F32)

        def put(j, r, value):
            CS[i, j, r : r + HALF, :] = value.astype(BF16)

        rounded_halves(w0, put)
        sib_copy(i).start()
        return carry

    lax.fori_loop(0, 8, step, 0)
    own(7)
    finish(7)

    for i in range(0, 3):
        y1_first(i)
    for d in range(2):
        z1_take(d, 1)
    for i in range(3, 8):
        y1_first(i)
    y1_last(0)
    for d in range(2):
        z2_copy(d, 0).start()
    y1_last(1)
    for d in range(2):
        z1_take(d, 2)
    y1_last(2)
    for d in range(2):
        z2_take(d, 0)
    y1_last(3)
    y1_last(4)
    for d in range(2):
        z2_take(d, 1)
    for d in range(2):
        z1_take(d, 3)
    for d in range(2):
        y2_copy(d, 0).start()
    y1_last(5)
    for d in range(2):
        y2_copy(d, 0).wait_recv()
        S[7, QCHAIN[d][1], low, half(d)] += RY20[d]
        y2_copy(d, 1).start()
    y1_last(6)
    for d in range(2):
        z2_take(d, 2)
    y1_last(7)
    for d in range(2):
        y2_copy(d, 1).wait_recv()
    S[7, 3, low, :] += RY21[0] + RY21[1]
    for d in range(2):
        z2_take(d, 3)

    part = S[7, 3]
    scale, inverse = scale_pair(jnp.max(jnp.abs(part), axis=0, keepdims=True), 31)
    value = jnp.floor(part * inverse + 0.5) * scale
    for r in range(1, TILES):
        XC[r] = value[:, r * BLOCK : (r + 1) * BLOCK].astype(BF16)
        x_copy(r).start()
    total = value[:, :BLOCK]
    for r in range(1, TILES):
        x_copy(r).wait_recv()
        total = total + XR[r].astype(F32)

    result = jnp.dot(
        total.T, signs(True), preferred_element_type=F32, precision=lax.Precision.HIGHEST
    )
    OT[...] = result * factor
    for d in range(1, 8):
        f_copy(d).start()
    mine = pl.ds(pl.multiple_of(place * 16, 16), 16)
    columns = pl.ds(pl.multiple_of(place * BLOCK, BLOCK), BLOCK)
    OB[:, columns] = OT[mine, :]
    for d in range(1, 8):
        f_copy(d).wait_recv()
    out_ref[...] = OB[...]

    def drain(i, carry):
        sib_copy(i).wait_send()
        for d in range(2):
            for s in range(2):
                y1_copy(i, d, s).wait_send()
        return carry

    lax.fori_loop(0, 8, drain, 0)
    for d in range(2):
        for s in range(4):
            for u in range(2):
                z1_copy(d, s, u).wait_send()
            z2_copy(d, s).wait_send()
        for s in range(2):
            y2_copy(d, s).wait_send()
    for r in range(1, TILES):
        x_copy(r).wait_send()
    for d in range(1, 8):
        f_copy(d).wait_send()


def body(inputs, out_grads):
    tokens, din = inputs.shape
    width = out_grads.shape[1]
    everyone = lax.axis_size("hst") * lax.axis_size("chip")
    factor = 1.0 / (512.0 * math.sqrt(tokens * everyone))
    half_wide = WIDE // 2
    dma = pltpu.SemaphoreType.DMA
    return pl.pallas_call(
        functools.partial(kernel, factor),
        out_shape=jax.ShapeDtypeStruct((din // everyone, width), F32),
        in_specs=[pl.BlockSpec(memory_space=pl.ANY)] * 2,
        out_specs=pl.BlockSpec(memory_space=pltpu.VMEM),
        scratch_shapes=[
            pltpu.VMEM((8, tokens, WIDE), BF16),
            pltpu.VMEM((tokens, width), BF16),
            pltpu.VMEM((width, tokens), BF16),
            pltpu.VMEM((512, WIDE), F32),
            pltpu.VMEM((512, WIDE), F32),
            pltpu.VMEM((8, NY, BLOCK, WIDE), F32),
            pltpu.VMEM((8, NY, BLOCK, WIDE), BF16),
            pltpu.VMEM((8, NY, BLOCK, WIDE), BF16),
            pltpu.VMEM((2, 8, TALL, half_wide), F32),
            pltpu.VMEM((2, 8, TALL, WIDE), F32),
            pltpu.VMEM((2, 2, 2, SPLIT, half_wide), F32),
            pltpu.VMEM((2, 3, 2, 2, SPLIT, WIDE), F32),
            pltpu.VMEM((2, TALL, half_wide), F32),
            pltpu.VMEM((2, 3, TALL, WIDE), F32),
            pltpu.VMEM((2, SPLIT, half_wide), F32),
            pltpu.VMEM((2, SPLIT, WIDE), F32),
            pltpu.VMEM((TILES, BLOCK, BLOCK), BF16),
            pltpu.VMEM((TILES, BLOCK, BLOCK), BF16),
            pltpu.VMEM((BLOCK, BLOCK), F32),
            pltpu.VMEM((16, width), F32),
            dma((8, TILES)),
            dma,
            dma((8,)),
            dma((8,)),
            dma((2, 2, 8)),
            dma((2, 2, 8)),
            dma((2, 4, 2)),
            dma((2, 4, 2)),
            dma((2, 4)),
            dma((2, 4)),
            dma((2, 2)),
            dma((2, 2)),
            dma((TILES,)),
            dma((TILES,)),
            dma((8,)),
            dma((8,)),
        ],
        compiler_params=pltpu.CompilerParams(
            collective_id=0, has_side_effects=True, vmem_limit_bytes=60 * 2**20
        ),
        name="reduce_gradient",
    )(inputs, out_grads)


def solution(mesh):
    placed = (P(("hst", "chip"), None), P(("hst", "chip"), None))
    return jax.shard_map(
        body, mesh=mesh, in_specs=placed, out_specs=P(("hst", "chip"), None), check_vma=False
    )
```

time: 334 us -> 84.1 us (0.25)
  the two profiles are of different devices: /device:TPU:16 before, /device:TPU:1 now
where the time goes in v1:
time: 84.1 us; the launch traced here: 84 us
  Pallas kernels  82.5 us (98%)
  local copies, waits for them, and re-layouts  1.47 us (2%)
    pallas_call x1, Pallas kernels, body(): pl.pallas_call(functools.partial(kernel, factor), out_shape=jax.ShapeDtyp...  82.5 us

profile of v1, /device:TPU:1, one launch (start us, length us, event | category | flops | bytes accessed | tf_op | source)
XLA Modules:
  0.0 84.0 jit_solution(1598016355103615912)
XLA Ops:
  0.0 82.5 %reduce_gradient.1 = f32[16,1024]{1,0:T(8,128)} custom-call(bf16[1024,4096]{1,0:T(8,128)(2,1)} %a_ref.1, bf16[1024,1024]{1,0:T(8,128)(2,1)} %g_ref.1), custom_call_target="tpu_custom_call" | custom-call | tf_op jit(solution)/shard_map/reduce_gradient/pallas_call | solution.py:348
  82.5 1.5 %copy.4 = f32[16,1024]{1,0:T(8,128)} copy(f32[16,1024]{1,0:T(8,128)} %reduce_gradient.1) | data formatting | bytes 131072

commit v2 on v0

--- a/solution.py
+++ b/solution.py
@@ -1,9 +1,557 @@
+import functools
+import math
+
 import jax
 import jax.numpy as jnp
 from jax import lax
+from jax.experimental import pallas as pl
+from jax.experimental.pallas import tpu as pltpu
 from jax.sharding import PartitionSpec as P
 
+MESH = pl.DeviceIdType.MESH
+F32 = jnp.float32
+BF16 = jnp.bfloat16
 BLOCK = 128
+HALF = BLOCK // 2
+NX, NZ, NY, NK = 4, 8, 4, 2
+TILES = NX
+WIDE = TILES * BLOCK
+SPLIT = 48
+TALL = BLOCK - SPLIT
+CHAIN = ((0, 1, 3, 5, 7), (0, 2, 4, 6, 7))
+LAG = 2
+QCHAIN = ((0, 1, 3), (0, 2, 3))
+
+
+STEP = 80.0
+SPAN = 120.0
+FAR = 2.0**22
+
+
+def coded(number):
+    size = jnp.abs(number)
+    value = jnp.exp2(size - SPAN)
+    return jnp.where(number < 0, -value, value).astype(BF16), size
+
+
+def decoded(code, minus_unit):
+    value = code.astype(F32)
+    size = jnp.floor(jnp.log(jnp.abs(value)) * (STEP / math.log(2.0)) + (SPAN * STEP + 0.5))
+    return size * jnp.where(value < 0, minus_unit, -minus_unit)
+
+
+def signs(upper):
+    i = lax.broadcasted_iota(jnp.int32, (BLOCK, BLOCK), 0)
+    j = lax.broadcasted_iota(jnp.int32, (BLOCK, BLOCK), 1)
+    t = i & j
+    if not upper:
+        t = t & (HALF - 1)
+    t = t ^ (t >> 4)
+    t = t ^ (t >> 2)
+    t = t ^ (t >> 1)
+    value = (1 - 2 * (t & 1)).astype(F32)
+    if not upper:
+        value = jnp.where((i & HALF) == (j & HALF), value, 0.0)
+    return value
+
+
+def scale_pair(largest, count):
+    scale = jnp.full_like(largest, 1.0 / 128.0)
+    inverse = jnp.full_like(largest, 128.0)
+    for k in range(count):
+        above = largest >= 2.0**k
+        scale = jnp.where(above, 2.0 ** (k + 1) / 128.0, scale)
+        inverse = jnp.where(above, 128.0 / 2.0 ** (k + 1), inverse)
+    return scale, inverse
+
+
+def rounded_halves(w_ref, put, units):
+    tops = []
+    for j in range(NY):
+        u = w_ref[j * BLOCK : j * BLOCK + HALF]
+        v = w_ref[j * BLOCK + HALF : (j + 1) * BLOCK]
+        tops.append(jnp.max(jnp.abs(u) + jnp.abs(v), axis=0, keepdims=True))
+    largest = jnp.concatenate(tops, axis=0)
+    scale, inverse = scale_pair(largest, 22)
+    used = largest >= 1.0
+    minus = jnp.max(jnp.where(used, -scale, -FAR), axis=0, keepdims=True)
+    finest = jnp.max(jnp.where(used, inverse, 1.0 / FAR), axis=0, keepdims=True)
+    for h in range(TILES):
+        units[h : h + 1, :] = minus[:, h * BLOCK : (h + 1) * BLOCK]
+        units[8 + h : 9 + h, :] = finest[:, h * BLOCK : (h + 1) * BLOCK]
+    for j in range(NY):
+        s, inv = scale[j : j + 1], inverse[j : j + 1]
+        u = w_ref[j * BLOCK : j * BLOCK + HALF] * inv
+        v = w_ref[j * BLOCK + HALF : (j + 1) * BLOCK] * inv
+        put(j, 0, jnp.floor(u + v + 0.5) * s)
+        put(j, HALF, jnp.floor(u - v + 0.5) * s)
+
+
+def kernel(
+    factor, a_ref, g_ref, out_ref, bad_ref,
+    abuf, gbuf, gt, w0, w1, S, CS, CR, EY0, RY0, EY1, RY1, EZ0, RZ0, EZ1, RZ1, EZ20, RZ20, EZ21, RZ21,
+    EY20, RY20, EY21, RY21, XC, XR, FC, FR, UO, UT, UC, UY, UZ, FM,
+    a_sem, g_sem, sib_r, y1_r, z1_r, z2_r, y2_r, x_r, f_r, out_sem,
+):
+    x = lax.axis_index("hst")
+    c = lax.axis_index("chip")
+    z, y, k = c // 8, (c // 2) % 4, c % 2
+
+    def dev(x_, z_, y_, k_):
+        return (x_, (z_ * NY + y_) * NK + k_)
+
+    sibling = dev(x, z, y, 1 - k)
+    y_next = (dev(x, z, (y + 1) % 4, k), dev(x, z, (y + 3) % 4, k))
+    z_next = (dev(x, (z + 1) % 8, y, k), dev(x, (z + 7) % 8, y, k))
+    place = y * 2 + k
+
+    def owner(r, d):
+        return ((x + r) % 4, z * 8 + (place + d) % 8)
+
+    def along(d):
+        return (x, ((z + d) % 8) * 8 + place)
+
+    peers = [(r, d) for r in range(TILES) for d in range(8) if (r, d) != (0, 0)]
+
+    def g_copy():
+        return pltpu.make_async_copy(g_ref, gbuf, g_sem)
+
+    def a_copy(i, r):
+        off = jnp.where(i % 2 == 0, 4 + i // 2, 3 - i // 2)
+        start = (((x + r) % 4) * 8 + (z + off) % 8) * BLOCK
+        return pltpu.make_async_copy(
+            a_ref.at[:, pl.ds(pl.multiple_of(start, BLOCK), BLOCK)],
+            abuf.at[i, :, pl.ds(r * BLOCK, BLOCK)],
+            a_sem.at[i],
+        )
+
+    g_copy().start()
+
+    def start_a(i, carry):
+        for r in range(TILES):
+            a_copy(i, r).start()
+        return carry
+
+    lax.fori_loop(0, 8, start_a, 0)
+
+    barrier = pltpu.get_barrier_semaphore()
+    friends = [along(d) for d in range(1, 8)] + [owner(r, d) for r, d in peers]
+    for friend in friends:
+        pl.semaphore_signal(barrier, inc=1, device_id=friend, device_id_type=MESH)
+
+    def remote(src, dst, ss, rs, to):
+        return pltpu.make_async_remote_copy(
+            src_ref=src, dst_ref=dst, send_sem=ss, recv_sem=rs, device_id=to, device_id_type=MESH
+        )
+
+    def sib_copy(i):
+        return remote(CS.at[i], CR.at[i], out_sem.at[0], sib_r.at[i], sibling)
+
+    def y1_copy(i, d, s):
+        src, dst = (EY0, RY0) if s == 0 else (EY1, RY1)
+        return remote(src.at[d, i], dst.at[d, i], out_sem.at[1 + s], y1_r.at[d, s, i], y_next[d])
+
+    def z1_copy(d, s, u):
+        if s == 0:
+            src, dst = EZ0.at[d, u], RZ0.at[d, u]
+        else:
+            src, dst = EZ1.at[d, s - 1, u], RZ1.at[d, s - 1, u]
+        return remote(src, dst, out_sem.at[3 + min(s, 1)], z1_r.at[d, s, u], z_next[d])
+
+    def z2_copy(d, s):
+        if s == 0:
+            src, dst = EZ20.at[d], RZ20.at[d]
+        else:
+            src, dst = EZ21.at[d, s - 1], RZ21.at[d, s - 1]
+        return remote(src, dst, out_sem.at[5 + min(s, 1)], z2_r.at[d, s], z_next[d])
+
+    def y2_copy(d, s):
+        src, dst = (EY20, RY20) if s == 0 else (EY21, RY21)
+        return remote(src.at[d], dst.at[d], out_sem.at[7 + s], y2_r.at[d, s], y_next[d])
+
+    def f_copy(d):
+        return remote(FC, FR.at[d], out_sem.at[9], f_r, along(d))
+
+    def x_copy(r, d):
+        src = XC.at[r * 8 + (place + d) % 8]
+        return remote(src, XR.at[r * 8 + d], out_sem.at[10], x_r, owner(r, d))
+
+    def relay(count, row, items):
+        def one(t, top):
+            rows = pl.ds(pl.multiple_of(row + 16 * t, 16), 16)
+            for i, q, h, arrivals, leaving in items:
+                columns = slice(h * BLOCK, (h + 1) * BLOCK)
+                v = S[i, q, rows, columns]
+                for ref, base, stride, unit in arrivals:
+                    v = v + decoded(ref[base + stride * t], unit[h : h + 1])
+                if leaving is None:
+                    S[i, q, rows, columns] = v
+                else:
+                    ref, base, stride, unit = leaving
+                    code, size = coded(v * (unit[8 + h : 9 + h] * (1.0 / STEP)))
+                    ref[base + stride * t] = code
+                    top = jnp.maximum(top, size)
+            return top
+
+        FM[...] = lax.fori_loop(0, count, one, FM[...])
+
+    TR, LR = TALL // 16, SPLIT // 16
+
+    def unit_of(ref):
+        return ref[ref.shape[0] - 1].astype(F32)
+
+    def sign_unit(ref, unit):
+        ref[ref.shape[0] - 1] = unit.astype(BF16)
+
+    def y1_start(i):
+        unit = UC[i]
+        items = []
+        for d in range(2):
+            sign_unit(EY0.at[d, i], unit)
+            items += [(i, 0, 2 * d + e, [], (EY0.at[d, i], e, 2, unit)) for e in range(2)]
+        relay(TR, SPLIT, items)
+        for d in range(2):
+            y1_copy(i, d, 0).start()
+
+    def y1_first(i):
+        items = []
+        for d in range(2):
+            y1_copy(i, d, 0).wait_recv()
+            came = unit_of(RY0.at[d, i])
+            unit = jnp.maximum(UC[i], came)
+            sign_unit(EY1.at[d, i], unit)
+            for h in range(TILES):
+                arrivals = [(RY0.at[d, i], h % 2, 2, came)] if h // 2 == d else []
+                items.append((i, QCHAIN[d][1], h, arrivals, (EY1.at[d, i], h, TILES, unit)))
+        relay(TR, SPLIT, items)
+        for d in range(2):
+            y1_copy(i, d, 1).start()
+
+    def y1_last(i):
+        units = []
+        for d in range(2):
+            y1_copy(i, d, 1).wait_recv()
+            units.append(unit_of(RY1.at[d, i]))
+        arrivals = [[(RY1.at[d, i], h, TILES, units[d]) for d in range(2)] for h in range(TILES)]
+        relay(TR, SPLIT, [(i, 3, h, arrivals[h], None) for h in range(TILES)])
+        UY[i] = jnp.maximum(UC[i], jnp.maximum(units[0], units[1]))
+
+    def z1_start():
+        unit = UC[0]
+        for u in range(2):
+            items = []
+            for d in range(2):
+                sign_unit(EZ0.at[d, u], unit)
+                for q in range(2):
+                    for e in range(2):
+                        leaving = (EZ0.at[d, u], q * LR * 2 + e, 2, unit)
+                        items.append((0, 2 * u + q, 2 * d + e, [], leaving))
+            relay(LR, 0, items)
+            for d in range(2):
+                z1_copy(d, 0, u).start()
+
+    def z1_take(s, u):
+        for d in range(2):
+            z1_copy(d, s, u).wait_recv()
+            ref = RZ0.at[d, u] if s == 0 else RZ1.at[d, s - 1, u]
+            slot = CHAIN[d][s + 1]
+            came = unit_of(ref)
+            unit = jnp.maximum(UZ[slot], came)
+            items = []
+            for q in range(2):
+                for h in range(TILES):
+                    base = q * LR * TILES + h
+                    arrivals = [(ref, base, TILES, came)]
+                    if s == 0:
+                        arrivals = [(ref, q * LR * 2 + h % 2, 2, came)] if h // 2 == d else []
+                    leaving = (EZ1.at[d, s, u], base, TILES, unit) if s < 3 else None
+                    items.append((slot, 2 * u + q, h, arrivals, leaving))
+            if s < 3:
+                sign_unit(EZ1.at[d, s, u], unit)
+                relay(LR, 0, items)
+                z1_copy(d, s + 1, u).start()
+            else:
+                UZ[slot] = unit
+                relay(LR, 0, items)
+
+    def z2_start():
+        unit = UY[0]
+        items = []
+        for d in range(2):
+            sign_unit(EZ20.at[d], unit)
+            items += [(0, 3, 2 * d + e, [], (EZ20.at[d], e, 2, unit)) for e in range(2)]
+        relay(TR, SPLIT, items)
+        for d in range(2):
+            z2_copy(d, 0).start()
+
+    def z2_take(s):
+        for d in range(2):
+            z2_copy(d, s).wait_recv()
+            ref = RZ20.at[d] if s == 0 else RZ21.at[d, s - 1]
+            slot = CHAIN[d][s + 1]
+            came = unit_of(ref)
+            unit = jnp.maximum(UY[slot], came)
+            items = []
+            for h in range(TILES):
+                arrivals = [(ref, h, TILES, came)]
+                if s == 0:
+                    arrivals = [(ref, h % 2, 2, came)] if h // 2 == d else []
+                items.append((slot, 3, h, arrivals, (EZ21.at[d, s], h, TILES, unit) if s < 3 else None))
+            if s < 3:
+                sign_unit(EZ21.at[d, s], unit)
+            relay(TR, SPLIT, items)
+            if s < 3:
+                z2_copy(d, s + 1).start()
+
+    def y2_start():
+        unit = UZ[7]
+        items = []
+        for d in range(2):
+            sign_unit(EY20.at[d], unit)
+            items += [(7, 0, 2 * d + e, [], (EY20.at[d], e, 2, unit)) for e in range(2)]
+        relay(LR, 0, items)
+        for d in range(2):
+            y2_copy(d, 0).start()
+
+    def y2_first():
+        items = []
+        for d in range(2):
+            y2_copy(d, 0).wait_recv()
+            came = unit_of(RY20.at[d])
+            unit = jnp.maximum(UZ[7], came)
+            sign_unit(EY21.at[d], unit)
+            for h in range(TILES):
+                arrivals = [(RY20.at[d], h % 2, 2, came)] if h // 2 == d else []
+                items.append((7, QCHAIN[d][1], h, arrivals, (EY21.at[d], h, TILES, unit)))
+        relay(LR, 0, items)
+        for d in range(2):
+            y2_copy(d, 1).start()
+
+    def y2_last():
+        items = []
+        units = []
+        for d in range(2):
+            y2_copy(d, 1).wait_recv()
+            units.append(unit_of(RY21.at[d]))
+        for h in range(TILES):
+            items.append((7, 3, h, [(RY21.at[d], h, TILES, units[d]) for d in range(2)], None))
+        relay(LR, 0, items)
+
+    FM[...] = jnp.zeros_like(FM)
+    UT[...] = jnp.zeros_like(UT)
+    UO[...] = jnp.zeros_like(UO)
+
+    g_copy().wait()
+    table = signs(False).astype(BF16)
+    for h in range(2):
+        for q, off in enumerate((2, 1, 3, 0)):
+            block = ((y + off) % 4) * 2 + (1 - k if h == 0 else k)
+            columns = pl.ds(pl.multiple_of(block * BLOCK, BLOCK), BLOCK)
+            turned = lax.dot_general(
+                table, gbuf[:, columns], (((1,), (1,)), ((), ())), preferred_element_type=F32
+            )
+            start = h * 512 + q * BLOCK
+            gt[start : start + BLOCK, :] = turned.astype(BF16)
+
+    def own(i):
+        def put(j, r, value):
+            S[i, j, r : r + HALF, :] = value
+
+        rounded_halves(w1, put, UO.at[i])
+
+    def finish(i):
+        sib_copy(i).wait_recv()
+
+        def add(t, carry):
+            rows = pl.ds(pl.multiple_of(16 * t, 16), 16)
+            for q in range(NY):
+                for h in range(TILES):
+                    columns = slice(h * BLOCK, (h + 1) * BLOCK)
+                    S[i, q, rows, columns] += CR[i, (q * TILES + h) * 8 + t].astype(F32)
+            return carry
+
+        lax.fori_loop(0, 8, add, 0)
+        unit = jnp.maximum(UO[i], unit_of(CR.at[i]))
+        UC[i] = unit
+        UZ[i] = unit
+        y1_start(i)
+
+    def multiply(i):
+        pltpu.make_async_copy(a_ref.at[:, pl.ds(0, WIDE)], abuf.at[i], a_sem.at[i]).wait()
+        w0[...] = jnp.dot(gt[0:512, :], abuf[i], preferred_element_type=F32)
+        own(jnp.maximum(i - 1, 0))
+
+    def multiply_more(i):
+        w1[...] = jnp.dot(gt[512:1024, :], abuf[i], preferred_element_type=F32)
+
+        def put(j, r, value):
+            for h in range(TILES):
+                for t in range(HALF // 16):
+                    tile = value[t * 16 : (t + 1) * 16, h * BLOCK : (h + 1) * BLOCK]
+                    CS[i, (j * TILES + h) * 8 + r // 16 + t] = tile.astype(BF16)
+
+        rounded_halves(w0, put, UT)
+        CS[i, NY * TILES * 8] = UT[...].astype(BF16)
+
+    def step(i, carry):
+        multiply(i)
+
+        @pl.when(i >= LAG)
+        def _():
+            finish(i - LAG)
+
+        @pl.when(i == LAG)
+        def _():
+            z1_start()
+
+        @pl.when(i >= LAG + 2)
+        def _():
+            y1_first(i - LAG - 2)
+
+        @pl.when(i == LAG + 4)
+        def _():
+            for u in range(2):
+                z1_take(0, u)
+
+        multiply_more(i)
+        sib_copy(i).start()
+        return carry
+
+    multiply(0)
+    multiply_more(0)
+    pl.semaphore_wait(barrier, len(friends))
+    sib_copy(0).start()
+    lax.fori_loop(1, 8, step, 0)
+    own(7)
+    z1_take(1, 0)
+    y1_last(0)
+    z2_start()
+    finish(6)
+    z1_take(1, 1)
+    y1_first(4)
+    y1_last(1)
+    finish(7)
+    y1_first(5)
+    y1_last(2)
+    z2_take(0)
+    z1_take(2, 0)
+    y1_first(6)
+    y1_last(3)
+    z1_take(2, 1)
+    y1_first(7)
+    y1_last(4)
+    z2_take(1)
+    z1_take(3, 0)
+    y1_last(5)
+    z1_take(3, 1)
+    y2_start()
+    y1_last(6)
+    z2_take(2)
+    y2_first()
+    FC[...] = FM[...]
+    for d in range(1, 8):
+        f_copy(d).start()
+    y1_last(7)
+    z2_take(3)
+    y2_last()
+
+    part = S[7, 3]
+    scale, inverse = scale_pair(jnp.max(jnp.abs(part), axis=0, keepdims=True), 31)
+    value = (jnp.floor(part * inverse + 0.5) * scale).T
+    top = FM[...]
+    remote(FR.at[pl.ds(1, 7)], FR.at[pl.ds(1, 7)], out_sem.at[9], f_r, sibling).wait_recv()
+    for d in range(1, 8):
+        top = jnp.maximum(top, FR[d])
+    bad = jnp.where(top <= 2 * SPAN, 0.0, 1.0).astype(BF16)
+    for r in range(TILES):
+        for g in range(8):
+            start = r * BLOCK + g * 16
+            XC[r * 8 + g, 0:16] = value[start : start + 16].astype(BF16)
+            XC[r * 8 + g, 16:32] = bad
+    for r, d in peers:
+        x_copy(r, d).start()
+    XR[0] = XC[place]
+
+    gone = (CS, EY0, EY1, EZ0, EZ1, EZ20, EZ21, EY20, EY21, FR.at[pl.ds(1, 7)])
+    for n, ref in enumerate(gone):
+        remote(ref, ref, out_sem.at[n], x_r, sibling).wait_send()
+
+    remaining = pl.ds(1, TILES * 8 - 1)
+    remote(XR.at[remaining], XR.at[remaining], out_sem.at[10], x_r, sibling).wait_recv()
+    total = XR[0:8, 0:16].astype(F32)
+    for r in range(1, TILES):
+        total = total + XR[r * 8 : r * 8 + 8, 0:16].astype(F32)
+    flags = XR[:, 16:32].astype(F32).reshape(TILES * 8 * 16, BLOCK)
+    bad_ref[...] = jnp.full_like(bad_ref, jnp.max(flags))
+    result = jnp.dot(
+        total.reshape(BLOCK, BLOCK), signs(True),
+        preferred_element_type=F32, precision=lax.Precision.HIGHEST,
+    ) * factor
+    for d in range(8):
+        columns = pl.ds(pl.multiple_of(((place + 8 - d) % 8) * BLOCK, BLOCK), BLOCK)
+        out_ref[:, columns] = result[d * 16 : (d + 1) * 16]
+    remote(XR.at[remaining], XR.at[remaining], out_sem.at[10], x_r, sibling).wait_send()
+
+
+def quick(inputs, out_grads):
+    tokens, din = inputs.shape
+    width = out_grads.shape[1]
+    everyone = lax.axis_size("hst") * lax.axis_size("chip")
+    factor = 1.0 / (512.0 * math.sqrt(tokens * everyone))
+    tall, low = TALL // 16 * TILES, SPLIT // 16 * TILES
+    dma = pltpu.SemaphoreType.DMA
+
+    def tiles(*shape):
+        return [pltpu.VMEM(shape + (16, BLOCK), BF16)]
+
+    def both(*shape):
+        return tiles(*shape) * 2
+
+    unit = pltpu.VMEM((8, 16, BLOCK), F32)
+    return pl.pallas_call(
+        functools.partial(kernel, factor),
+        out_shape=(
+            jax.ShapeDtypeStruct((din // everyone, width), F32),
+            jax.ShapeDtypeStruct((8, BLOCK), F32),
+        ),
+        in_specs=[pl.BlockSpec(memory_space=pl.ANY)] * 2,
+        out_specs=[pl.BlockSpec(memory_space=pltpu.VMEM)] * 2,
+        scratch_shapes=[
+            pltpu.VMEM((8, tokens, WIDE), BF16),
+            pltpu.VMEM((tokens, width), BF16),
+            pltpu.VMEM((width, tokens), BF16),
+            pltpu.VMEM((512, WIDE), F32),
+            pltpu.VMEM((512, WIDE), F32),
+            pltpu.VMEM((8, NY, BLOCK, WIDE), F32),
+        ]
+        + both(8, NY * TILES * 8 + 1)
+        + both(2, 8, tall // 2 + 1)
+        + both(2, 8, tall + 1)
+        + both(2, 2, low + 1)
+        + both(2, 3, 2, 2 * low + 1)
+        + both(2, tall // 2 + 1)
+        + both(2, 3, tall + 1)
+        + both(2, low // 2 + 1)
+        + both(2, low + 1)
+        + [
+            pltpu.VMEM((TILES * 8, 32, BLOCK), BF16),
+            pltpu.VMEM((TILES * 8, 32, BLOCK), BF16),
+            pltpu.VMEM((16, BLOCK), F32),
+            pltpu.VMEM((8, 16, BLOCK), F32),
+            unit,
+            pltpu.VMEM((16, BLOCK), F32),
+            unit,
+            unit,
+            unit,
+            pltpu.VMEM((16, BLOCK), F32),
+        ]
+        + [dma((8,)), dma, dma((8,)), dma((2, 2, 8)), dma((2, 4, 2)), dma((2, 4)), dma((2, 2))]
+        + [dma, dma, dma((11,))],
+        compiler_params=pltpu.CompilerParams(
+            collective_id=0, has_side_effects=True, vmem_limit_bytes=60 * 2**20
+        ),
+        name="reduce_gradient",
+    )(inputs, out_grads)
 
 
 powers_list = [2.0**k for k in range(31)]
@@ -36,7 +584,7 @@
     return codes.astype(jnp.float32) * scales[..., None]
 
 
-def body(inputs, out_grads):
+def plain(inputs, out_grads):
     table = hadamard_table(BLOCK)
     hosts = lax.axis_size("hst")
     chips = lax.axis_size("chip")
@@ -79,6 +627,11 @@
     return result.reshape(rows, width) * factor
 
 
+def body(inputs, out_grads):
+    result, bad = quick(inputs, out_grads)
+    return lax.cond(bad[0, 0] > 0, plain, lambda a, b: result, inputs, out_grads)
+
+
 def solution(mesh):
     placed = (P(("hst", "chip"), None), P(("hst", "chip"), None))
     return jax.shard_map(

time: 334 us -> 63.1 us (0.19)
  the two profiles are of different devices: /device:TPU:16 before, /device:TPU:1 now
where the time goes in v2:
time: 63.1 us; the launch traced here: 63 us
  Pallas kernels  60.2 us (95%)
  local copies, waits for them, and re-layouts  1.83 us (3%)
  between operations  0.68 us (1%)
    pallas_call x1, Pallas kernels, quick(): pl.pallas_call(functools.partial(kernel, factor), out_shape=(jax.ShapeDty...  60.2 us

profile of v2, /device:TPU:1, one launch (start us, length us, event | category | flops | bytes accessed | tf_op | source)
XLA Modules:
  0.0 63.0 jit_solution(2608554212174788906)
XLA Ops:
  0.0 0.0 copy-start
  0.0 60.2 %reduce_gradient.1 = (f32[16,1024]{1,0:T(8,128)S(1)}, f32[8,128]{1,0:T(8,128)}) custom-call(bf16[1024,4096]{1,0:T(8,128)(2,1)} %a_ref.1, bf16[1024,1024]{1,0:T(8,128)(2,1)} %g_ref.1), custom_call_target="tpu_custom_call" | custom-call | tf_op jit(solution)/shard_map/reduce_gradient/pallas_call | solution.py:511
  60.3 1.2 %slice.3 = f32[1,1]{1,0:T(1,128)} slice(f32[8,128]{1,0:T(8,128)} %get-tuple-element.29), slice={[0:1], [0:1]} | slice | bytes 8 | tf_op jit(solution)/shard_map/slice | solution.py:632
  62.1 0.0 copy-done
  62.1 0.2 conditional.1
  62.3 0.6 %copy.56 = f32[16,1024]{1,0:T(8,128)} copy(f32[16,1024]{1,0:T(8,128)S(1)} %get-tuple-element.31) | data formatting | bytes 131072
Async XLA Ops:
  0.0 62.1 %copy-start = (bf16[1024,1024]{1,0:T(8,128)(2,1)S(1)}, bf16[1024,1024]{1,0:T(8,128)(2,1)}, u32[]{:S(2)}) copy-start(bf16[1024,1024]{1,0:T(8,128)(2,1)} %g_ref.1) | copy-start | bytes 6291460

commit v3 on v2

--- a/solution.py
+++ b/solution.py
@@ -19,7 +19,7 @@
 SPLIT = 48
 TALL = BLOCK - SPLIT
 CHAIN = ((0, 1, 3, 5, 7), (0, 2, 4, 6, 7))
-LAG = 2
+LAG = 3
 QCHAIN = ((0, 1, 3), (0, 2, 3))
 
 
@@ -112,9 +112,17 @@
         return (x, ((z + d) % 8) * 8 + place)
 
     peers = [(r, d) for r in range(TILES) for d in range(8) if (r, d) != (0, 0)]
-
-    def g_copy():
-        return pltpu.make_async_copy(g_ref, gbuf, g_sem)
+    peers.sort(key=lambda p: -2 * min(p[0], TILES - p[0]) - min(p[1], 8 - p[1]))
+
+    def kv_columns(h, q):
+        block = ((y + (2, 1, 3, 0)[q]) % 4) * 2 + (1 - k if h == 0 else k)
+        return pl.ds(pl.multiple_of(block * BLOCK, BLOCK), BLOCK)
+
+    def g_copy(h, q):
+        start = h * 512 + q * BLOCK
+        return pltpu.make_async_copy(
+            g_ref.at[:, kv_columns(h, q)], gbuf.at[:, pl.ds(start, BLOCK)], g_sem.at[h]
+        )
 
     def a_copy(i, r):
         off = jnp.where(i % 2 == 0, 4 + i // 2, 3 - i // 2)
@@ -125,14 +133,14 @@
             a_sem.at[i],
         )
 
-    g_copy().start()
-
     def start_a(i, carry):
         for r in range(TILES):
             a_copy(i, r).start()
         return carry
 
-    lax.fori_loop(0, 8, start_a, 0)
+    for q in range(NY):
+        g_copy(0, q).start()
+    start_a(0, 0)
 
     barrier = pltpu.get_barrier_semaphore()
     friends = [along(d) for d in range(1, 8)] + [owner(r, d) for r, d in peers]
@@ -193,7 +201,7 @@
                     top = jnp.maximum(top, size)
             return top
 
-        FM[...] = lax.fori_loop(0, count, one, FM[...])
+        FM[...] = lax.fori_loop(0, count, one, FM[...], unroll=True)
 
     TR, LR = TALL // 16, SPLIT // 16
 
@@ -202,16 +210,6 @@
 
     def sign_unit(ref, unit):
         ref[ref.shape[0] - 1] = unit.astype(BF16)
-
-    def y1_start(i):
-        unit = UC[i]
-        items = []
-        for d in range(2):
-            sign_unit(EY0.at[d, i], unit)
-            items += [(i, 0, 2 * d + e, [], (EY0.at[d, i], e, 2, unit)) for e in range(2)]
-        relay(TR, SPLIT, items)
-        for d in range(2):
-            y1_copy(i, d, 0).start()
 
     def y1_first(i):
         items = []
@@ -341,49 +339,63 @@
     UT[...] = jnp.zeros_like(UT)
     UO[...] = jnp.zeros_like(UO)
 
-    g_copy().wait()
     table = signs(False).astype(BF16)
-    for h in range(2):
-        for q, off in enumerate((2, 1, 3, 0)):
-            block = ((y + off) % 4) * 2 + (1 - k if h == 0 else k)
-            columns = pl.ds(pl.multiple_of(block * BLOCK, BLOCK), BLOCK)
+
+    def turn(h):
+        half_columns = pl.ds(h * 512, 512)
+        pltpu.make_async_copy(
+            g_ref.at[:, half_columns], gbuf.at[:, half_columns], g_sem.at[h]
+        ).wait()
+        for q in range(NY):
+            start = h * 512 + q * BLOCK
             turned = lax.dot_general(
-                table, gbuf[:, columns], (((1,), (1,)), ((), ())), preferred_element_type=F32
+                table, gbuf[:, start : start + BLOCK], (((1,), (1,)), ((), ())),
+                preferred_element_type=F32,
             )
-            start = h * 512 + q * BLOCK
             gt[start : start + BLOCK, :] = turned.astype(BF16)
 
-    def own(i):
+    def finish(i):
+        came = unit_of(CR.at[i])
+        unit = [None]
+        tops = [FM[...]]
+
         def put(j, r, value):
-            S[i, j, r : r + HALF, :] = value
-
-        rounded_halves(w1, put, UO.at[i])
-
-    def finish(i):
-        sib_copy(i).wait_recv()
-
-        def add(t, carry):
-            rows = pl.ds(pl.multiple_of(16 * t, 16), 16)
-            for q in range(NY):
+            if unit[0] is None:
+                unit[0] = jnp.maximum(UO[...], came)
+            for t in range(HALF // 16):
+                row = r + t * 16
                 for h in range(TILES):
-                    columns = slice(h * BLOCK, (h + 1) * BLOCK)
-                    S[i, q, rows, columns] += CR[i, (q * TILES + h) * 8 + t].astype(F32)
-            return carry
-
-        lax.fori_loop(0, 8, add, 0)
-        unit = jnp.maximum(UO[i], unit_of(CR.at[i]))
-        UC[i] = unit
-        UZ[i] = unit
-        y1_start(i)
-
-    def multiply(i):
+                    tile = value[t * 16 : (t + 1) * 16, h * BLOCK : (h + 1) * BLOCK]
+                    tile = tile + CR[i, (j * TILES + h) * 8 + row // 16].astype(F32)
+                    if j == 0 and row >= SPLIT:
+                        inverse = unit[0][8 + h : 9 + h] * (1.0 / STEP)
+                        code, size = coded(tile * inverse)
+                        EY0[h // 2, i, (row - SPLIT) // 16 * 2 + h % 2] = code
+                        tops[0] = jnp.maximum(tops[0], size)
+                    else:
+                        S[i, j, row : row + 16, h * BLOCK : (h + 1) * BLOCK] = tile
+
+        rounded_halves(w1.at[i % (LAG + 1)], put, UO)
+        FM[...] = tops[0]
+        UC[i] = unit[0]
+        UZ[i] = unit[0]
+        for d in range(2):
+            sign_unit(EY0.at[d, i], unit[0])
+
+    def leave(i):
+        for d in range(2):
+            y1_copy(i, d, 0).start()
+
+    def landed(i):
         pltpu.make_async_copy(a_ref.at[:, pl.ds(0, WIDE)], abuf.at[i], a_sem.at[i]).wait()
+
+    def multiply_sent(i):
         w0[...] = jnp.dot(gt[0:512, :], abuf[i], preferred_element_type=F32)
-        own(jnp.maximum(i - 1, 0))
-
-    def multiply_more(i):
-        w1[...] = jnp.dot(gt[512:1024, :], abuf[i], preferred_element_type=F32)
-
+
+    def multiply_kept(i):
+        w1[i % (LAG + 1)] = jnp.dot(gt[512:1024, :], abuf[i], preferred_element_type=F32)
+
+    def round_sent(i):
         def put(j, r, value):
             for h in range(TILES):
                 for t in range(HALF // 16):
@@ -394,11 +406,11 @@
         CS[i, NY * TILES * 8] = UT[...].astype(BF16)
 
     def step(i, carry):
-        multiply(i)
-
-        @pl.when(i >= LAG)
-        def _():
-            finish(i - LAG)
+        landed(i)
+        sib_copy(i - LAG).wait_recv()
+        multiply_sent(i)
+        finish(i - LAG)
+        leave(i - LAG)
 
         @pl.when(i == LAG)
         def _():
@@ -408,68 +420,92 @@
         def _():
             y1_first(i - LAG - 2)
 
-        @pl.when(i == LAG + 4)
+        @pl.when(i == LAG + 2)
         def _():
             for u in range(2):
                 z1_take(0, u)
 
-        multiply_more(i)
+        @pl.when(i == 7)
+        def _():
+            z1_take(1, 0)
+
+        multiply_kept(i)
+        round_sent(i)
         sib_copy(i).start()
         return carry
 
-    multiply(0)
-    multiply_more(0)
+    turn(0)
+    for q in range(NY):
+        g_copy(1, q).start()
+    lax.fori_loop(1, 8, start_a, 0)
+    landed(0)
+    multiply_sent(0)
+    round_sent(0)
     pl.semaphore_wait(barrier, len(friends))
     sib_copy(0).start()
-    lax.fori_loop(1, 8, step, 0)
-    own(7)
-    z1_take(1, 0)
+    turn(1)
+    multiply_kept(0)
+    for i in range(1, LAG):
+        landed(i)
+        multiply_sent(i)
+        round_sent(i)
+        sib_copy(i).start()
+        multiply_kept(i)
+    lax.fori_loop(LAG, 8, step, 0)
+    def late(i):
+        sib_copy(i).wait_recv()
+        finish(i)
+        leave(i)
+
+    z1_take(1, 1)
     y1_last(0)
     z2_start()
-    finish(6)
-    z1_take(1, 1)
+    y1_first(3)
+    late(5)
+    y1_last(1)
+    late(6)
     y1_first(4)
-    y1_last(1)
-    finish(7)
+    y1_last(2)
+    z1_take(2, 0)
+    late(7)
+    z2_take(0)
     y1_first(5)
-    y1_last(2)
-    z2_take(0)
-    z1_take(2, 0)
-    y1_first(6)
     y1_last(3)
     z1_take(2, 1)
-    y1_first(7)
+    y1_first(6)
     y1_last(4)
     z2_take(1)
+    y1_first(7)
     z1_take(3, 0)
     y1_last(5)
     z1_take(3, 1)
     y2_start()
     y1_last(6)
     z2_take(2)
+    y1_last(7)
     y2_first()
     FC[...] = FM[...]
     for d in range(1, 8):
         f_copy(d).start()
-    y1_last(7)
     z2_take(3)
     y2_last()
 
     part = S[7, 3]
     scale, inverse = scale_pair(jnp.max(jnp.abs(part), axis=0, keepdims=True), 31)
-    value = (jnp.floor(part * inverse + 0.5) * scale).T
+    value = jnp.floor(part * inverse + 0.5) * scale
     top = FM[...]
     remote(FR.at[pl.ds(1, 7)], FR.at[pl.ds(1, 7)], out_sem.at[9], f_r, sibling).wait_recv()
     for d in range(1, 8):
         top = jnp.maximum(top, FR[d])
     bad = jnp.where(top <= 2 * SPAN, 0.0, 1.0).astype(BF16)
-    for r in range(TILES):
+    for r in (2, 1, 3, 0):
+        turned = value[:, r * BLOCK : (r + 1) * BLOCK].T.astype(BF16)
         for g in range(8):
-            start = r * BLOCK + g * 16
-            XC[r * 8 + g, 0:16] = value[start : start + 16].astype(BF16)
+            XC[r * 8 + g, 0:16] = turned[g * 16 : (g + 1) * 16]
             XC[r * 8 + g, 16:32] = bad
-    for r, d in peers:
-        x_copy(r, d).start()
+        for p, d in peers:
+            if p == r:
+                x_copy(r, d).start()
     XR[0] = XC[place]
 
     gone = (CS, EY0, EY1, EZ0, EZ1, EZ20, EZ21, EY20, EY21, FR.at[pl.ds(1, 7)])
@@ -521,7 +557,7 @@
             pltpu.VMEM((tokens, width), BF16),
             pltpu.VMEM((width, tokens), BF16),
             pltpu.VMEM((512, WIDE), F32),
-            pltpu.VMEM((512, WIDE), F32),
+            pltpu.VMEM((LAG + 1, 512, WIDE), F32),
             pltpu.VMEM((8, NY, BLOCK, WIDE), F32),
         ]
         + both(8, NY * TILES * 8 + 1)
@@ -538,14 +574,14 @@
             pltpu.VMEM((TILES * 8, 32, BLOCK), BF16),
             pltpu.VMEM((16, BLOCK), F32),
             pltpu.VMEM((8, 16, BLOCK), F32),
-            unit,
+            pltpu.VMEM((16, BLOCK), F32),
             pltpu.VMEM((16, BLOCK), F32),
             unit,
             unit,
             unit,
             pltpu.VMEM((16, BLOCK), F32),
         ]
-        + [dma((8,)), dma, dma((8,)), dma((2, 2, 8)), dma((2, 4, 2)), dma((2, 4)), dma((2, 2))]
+        + [dma((8,)), dma((2,)), dma((8,)), dma((2, 2, 8)), dma((2, 4, 2)), dma((2, 4)), dma((2, 2))]
         + [dma, dma, dma((11,))],
         compiler_params=pltpu.CompilerParams(
             collective_id=0, has_side_effects=True, vmem_limit_bytes=60 * 2**20

time: 63.1 us -> 59.1 us (0.937)
  Pallas kernels: 60.2 us -> 56.2 us
    pallas_call x1, Pallas kernels: 60.2 us -> 56.2 us  [quick(): pl.pallas_call(functools.partial(kernel, factor), out_shape=(jax.ShapeDty...]
where the time goes in v3:
time: 59.1 us; the launch traced here: 59 us
  Pallas kernels  56.2 us (95%)
  local copies, waits for them, and re-layouts  1.83 us (3%)
  between operations  0.68 us (1%)
    pallas_call x1, Pallas kernels, quick(): pl.pallas_call(functools.partial(kernel, factor), out_shape=(jax.ShapeDty...  56.2 us
    slice x1, local copies, waits for them, and re-layouts, body(): bad[0, 0] > 0  1.19 us

profile of v3, /device:TPU:1, one launch (start us, length us, event | category | flops | bytes accessed | tf_op | source)
XLA Modules:
  0.0 59.0 jit_solution(3487343945072386427)
XLA Ops:
  0.0 0.0 copy-start
  0.0 56.2 %reduce_gradient.1 = (f32[16,1024]{1,0:T(8,128)S(1)}, f32[8,128]{1,0:T(8,128)}) custom-call(bf16[1024,4096]{1,0:T(8,128)(2,1)} %a_ref.1, bf16[1024,1024]{1,0:T(8,128)(2,1)} %g_ref.1), custom_call_target="tpu_custom_call" | custom-call | tf_op jit(solution)/shard_map/reduce_gradient/pallas_call | solution.py:547
  56.2 1.2 %slice.3 = f32[1,1]{1,0:T(1,128)} slice(f32[8,128]{1,0:T(8,128)} %get-tuple-element.29), slice={[0:1], [0:1]} | slice | bytes 8 | tf_op jit(solution)/shard_map/slice | solution.py:668
  58.1 0.0 copy-done
  58.1 0.3 conditional.1
  58.3 0.6 %copy.56 = f32[16,1024]{1,0:T(8,128)} copy(f32[16,1024]{1,0:T(8,128)S(1)} %get-tuple-element.31) | data formatting | bytes 131072
Async XLA Ops:
  0.0 58.1 %copy-start = (bf16[1024,1024]{1,0:T(8,128)(2,1)S(1)}, bf16[1024,1024]{1,0:T(8,128)(2,1)}, u32[]{:S(2)}) copy-start(bf16[1024,1024]{1,0:T(8,128)(2,1)} %g_ref.1) | copy-start | bytes 6291460

commit v4 on v3

--- a/solution.py
+++ b/solution.py
@@ -154,6 +154,11 @@
 
     def sib_copy(i):
         return remote(CS.at[i], CR.at[i], out_sem.at[0], sib_r.at[i], sibling)
+
+    def sib_start(i):
+        for part, size in ((0, 33), (33, 32), (65, 32), (97, 32)):
+            tiles = pl.ds(part, size)
+            remote(CS.at[i, tiles], CR.at[i, tiles], out_sem.at[0], sib_r.at[i], sibling).start()
 
     def y1_copy(i, d, s):
         src, dst = (EY0, RY0) if s == 0 else (EY1, RY1)
@@ -431,7 +436,7 @@
 
         multiply_kept(i)
         round_sent(i)
-        sib_copy(i).start()
+        sib_start(i)
         return carry
 
     turn(0)
@@ -442,14 +447,14 @@
     multiply_sent(0)
     round_sent(0)
     pl.semaphore_wait(barrier, len(friends))
-    sib_copy(0).start()
+    sib_start(0)
     turn(1)
     multiply_kept(0)
     for i in range(1, LAG):
         landed(i)
         multiply_sent(i)
         round_sent(i)
-        sib_copy(i).start()
+        sib_start(i)
         multiply_kept(i)
     lax.fori_loop(LAG, 8, step, 0)
     def late(i):

time: 59.1 us -> 59.2 us (level)
  no operation moved by 1% of the time
where the time goes in v4:
time: 59.2 us; the launch traced here: 59.1 us
  Pallas kernels  56.3 us (95%)
  local copies, waits for them, and re-layouts  1.83 us (3%)
  between operations  0.68 us (1%)
    pallas_call x1, Pallas kernels, quick(): pl.pallas_call(functools.partial(kernel, factor), out_shape=(jax.ShapeDty...  56.3 us
    slice x1, local copies, waits for them, and re-layouts, body(): bad[0, 0] > 0  1.19 us

profile of v4, /device:TPU:1, one launch (start us, length us, event | category | flops | bytes accessed | tf_op | source)
XLA Modules:
  0.0 59.1 jit_solution(3977807814023165083)
XLA Ops:
  0.0 0.0 copy-start
  0.0 56.3 %reduce_gradient.1 = (f32[16,1024]{1,0:T(8,128)S(1)}, f32[8,128]{1,0:T(8,128)}) custom-call(bf16[1024,4096]{1,0:T(8,128)(2,1)} %a_ref.1, bf16[1024,1024]{1,0:T(8,128)(2,1)} %g_ref.1), custom_call_target="tpu_custom_call" | custom-call | tf_op jit(solution)/shard_map/reduce_gradient/pallas_call | solution.py:552
  56.3 1.2 %slice.3 = f32[1,1]{1,0:T(1,128)} slice(f32[8,128]{1,0:T(8,128)} %get-tuple-element.29), slice={[0:1], [0:1]} | slice | bytes 8 | tf_op jit(solution)/shard_map/slice | solution.py:673
  58.2 0.0 copy-done
  58.2 0.3 conditional.1
  58.5 0.6 %copy.56 = f32[16,1024]{1,0:T(8,128)} copy(f32[16,1024]{1,0:T(8,128)S(1)} %get-tuple-element.31) | data formatting | bytes 131072
Async XLA Ops:
  0.0 58.2 %copy-start = (bf16[1024,1024]{1,0:T(8,128)(2,1)S(1)}, bf16[1024,1024]{1,0:T(8,128)(2,1)}, u32[]{:S(2)}) copy-start(bf16[1024,1024]{1,0:T(8,128)(2,1)} %g_ref.1) | copy-start | bytes 6291460
